TPU v7x, 128 devices: a whole 4x4x4 slice. The times are simulated.
128 devices in a mesh: rep: 16 (over y, z_hi, core), shard: 8 (over x, z_lo).
Axes of the slice: x: 4, y: 4, z: 4 (z_hi: 2, z_lo: 2; z = z_hi * 2 + z_lo), core: 2. Of those that a mesh axis runs over, the one named last changes fastest.
Arguments:
- tokens: bfloat16 [16384, 2048], P(('rep', 'shard')), may hold values from -6 to 6
- out_cotangent: bfloat16 [16384, 2048], P(('rep', 'shard')), may hold values from -6 to 6
- attend_weight: bfloat16 [2048, 6144], P('shard'), may hold values from -0.125 to 0.125
- attend_bias: bfloat16 [6144], P('shard'), may hold values from -3 to 3
- dense_weight: bfloat16 [2048, 2048], P('shard'), may hold values from -0.75 to 0.75
- dense_bias: bfloat16 [2048], P('shard'), may hold values from -3 to 3
- expand_weight: bfloat16 [2048, 8192], P('shard'), may hold values from -0.125 to 0.125
- expand_bias: bfloat16 [8192], P('shard'), may hold values from -3 to 3
- shrink_weight: bfloat16 [8192, 2048], P('shard'), may hold values from -0.0625 to 0.0625
- shrink_bias: bfloat16 [2048], P('shard'), may hold values from -3 to 3
- attend_gain: bfloat16 [2048], P('shard'), may hold values from 0.25 to 1.75
- attend_shift: bfloat16 [2048], P('shard'), may hold values from -3 to 3
- feed_gain: bfloat16 [2048], P('shard'), may hold values from 0.25 to 1.75
- feed_shift: bfloat16 [2048], P('shard'), may hold values from -3 to 3
- lengths: int32 [16, 4], P('rep'), may hold values from 85 to 512, as said below
- slot_source: int32 [16, 1024], P('rep'), may hold values from 0 to 1023, as said below
Outputs:
- layer_out: bfloat16 [16384, 2048], P(('rep', 'shard'))
- tokens_gradient: float32 [16384, 2048], P(('rep', 'shard'))
- attend_weight_gradient: float32 [2048, 6144], P('shard')
- attend_bias_gradient: float32 [6144], P('shard')
- dense_weight_gradient: float32 [2048, 2048], P('shard')
- dense_bias_gradient: float32 [2048], P('shard')
- expand_weight_gradient: float32 [2048, 8192], P('shard')
- expand_bias_gradient: float32 [8192], P('shard')
- shrink_weight_gradient: float32 [8192, 2048], P('shard')
- shrink_bias_gradient: float32 [2048], P('shard')
- attend_gain_gradient: float32 [2048], P('shard')
- attend_shift_gradient: float32 [2048], P('shard')
- feed_gain_gradient: float32 [2048], P('shard')
- feed_shift_gradient: float32 [2048], P('shard')
Inputs may be any that keep to these rules, and one draw needn't show every extreme that they name: `lengths`: each row sums to 1024; the first sequence of every group has 512 tokens. `slot_source`: each row is a permutation of the group's packed indices; each row's slots are spread over the group's devices, 128 to a device.
All inputs are finite; a program needn't handle non-finite values.
Results may differ from a plain program's by a relative error of at most 0.024.
Values may be sent and summed in bfloat16 or wider, within the bound.
A program may use at most 448 MiB of HBM per device.

v0:
```python
import jax
import jax.numpy as jnp
from jax import lax
from jax.experimental import pallas as pl
from jax.experimental.pallas import tpu as pltpu
from jax.sharding import PartitionSpec as P

D = 2048
HD = 256
ROT = 64
FF_DEV = 1024
ROWS = 128
GROUP = 1024
EPSILON = 1e-05
NEG_FILL = -1e30
MESH = pl.DeviceIdType.MESH
BF = jnp.bfloat16
F32 = jnp.float32
NN = (((1,), (0,)), ((), ()))
NT = (((1,), (1,)), ((), ()))
TN = (((0,), (0,)), ((), ()))
INV_ROOT = HD ** (-0.5)


def dot(a, b, dims):
    return lax.dot_general(a, b, dims, preferred_element_type=F32)


def span(lo, hi, size, body):
    def step(i, carry):
        body(i, pl.ds(pl.multiple_of(i * size, size), size))
        return carry

    lax.fori_loop(lo, hi, step, 0)


def rows_at(start, count):
    return pl.ds(pl.multiple_of(start, 16), count)


def tiles(total, size, body):
    span(0, total // size, size, body)


def turn(values, cosine, sine):
    first = values[:, :128]
    lane = lax.broadcasted_iota(jnp.int32, first.shape, 1)
    swapped = jnp.where(lane < ROT // 2, pltpu.roll(first, 128 - ROT // 2, 1), pltpu.roll(first, ROT // 2, 1))
    return jnp.concatenate([first * cosine + swapped * sine, values[:, 128:]], axis=1)


class Links:
    def __init__(self, send_sems, recv_sems):
        self.rep, self.shard = lax.axis_index("rep"), lax.axis_index("shard")
        rep, shard = self.rep, self.shard
        self.y, self.zh, self.c = rep // 4, lax.rem(rep // 2, 2), lax.rem(rep, 2)
        self.x, self.zl = shard // 2, lax.rem(shard, 2)
        self.sibling = (self.y * 4 + self.zh * 2 + (1 - self.c), shard)
        self.z_rep = (self.y * 4 + (1 - self.zh) * 2 + self.c, shard)
        self.y_plus, self.y_minus, self.y_far = self.at_y(1), self.at_y(3), self.at_y(2)
        self.x_plus, self.x_minus = self.at_x(1), self.at_x(3)
        self.z_shard = (rep, self.x * 2 + (1 - self.zl))
        self.send_sems, self.recv_sems, self.used, self.open = send_sems, recv_sems, 0, []

    def at_y(self, step):
        return (lax.rem(self.y + step, 4) * 4 + self.zh * 2 + self.c, self.shard)

    def at_x(self, step):
        return (self.rep, lax.rem(self.x + step, 4) * 2 + self.zl)

    def peer(self, k):
        return lax.rem(self.shard + k, 8)

    def greet(self, devices, meanwhile=None):
        barrier = pltpu.get_barrier_semaphore()
        for device in devices:
            pl.semaphore_signal(barrier, inc=1, device_id=device, device_id_type=MESH)
        if meanwhile is not None:
            meanwhile()
        pl.semaphore_wait(barrier, len(devices))

    def send(self, src, dst, device):
        slot = self.used
        self.used += 1
        copy = pltpu.make_async_remote_copy(
            src_ref=src, dst_ref=dst, send_sem=self.send_sems.at[slot],
            recv_sem=self.recv_sems.at[slot], device_id=device, device_id_type=MESH,
        )
        copy.start()
        self.open.append(copy)
        return slot

    def move(self, src, dst):
        slot = self.used
        self.used += 1
        copy = pltpu.make_async_copy(src, dst, self.recv_sems.at[slot])
        copy.start()
        return slot

    def arrive(self, ref, slot):
        pltpu.make_async_copy(ref, ref, self.recv_sems.at[slot]).wait()

    def close(self):
        for copy in self.open:
            copy.wait_send()


def add_into(target, *others):
    count, total, width = target.shape
    size = 16
    while total % (2 * size) == 0 and 2 * size * width <= 65536:
        size *= 2

    def body(i, carry):
        rows = rows_at(lax.rem(i, total // size) * size, size)
        j = lax.div(i, total // size)
        value = target[j, rows, :].astype(F32)
        for other in others:
            value = value + other[j, rows, :].astype(F32)
        target[j, rows, :] = value.astype(BF)
        return carry

    lax.fori_loop(0, count * (total // size), body, 0)


def ring_steps(links, strip, local, near, far, pos, plus, minus):
    ahead, behind, across = lax.rem(pos + 1, 4), lax.rem(pos + 3, 4), lax.rem(pos + 2, 4)
    a = links.send(strip(across, 0), far.at[0], minus)
    b = links.send(strip(across, 1), far.at[1], plus)
    c0 = links.send(strip(behind, 1), near.at[0, :, 1], minus)
    c1 = links.send(strip(ahead, 0), near.at[1, :, 0], plus)
    yield
    links.arrive(far.at[0], a)
    below, above = local(behind, 0), local(ahead, 1)
    add_into(below, far.at[0])
    d0 = links.send(below, near.at[0, :, 0], minus)
    links.arrive(far.at[1], b)
    add_into(above, far.at[1])
    d1 = links.send(above, near.at[1, :, 1], plus)
    yield
    links.arrive(near.at[0, :, 1], c0)
    links.arrive(near.at[1, :, 0], c1)
    links.arrive(near.at[0, :, 0], d0)
    links.arrive(near.at[1, :, 1], d1)
    for h in range(2):
        add_into(local(pos, h), near.at[0, :, h], near.at[1, :, h])


def swap_steps(links, local, pos, other, index, partner):
    a = links.send(local(pos, 1 - index), other, partner)
    yield
    links.arrive(other, a)
    add_into(local(pos, index), other)


def token_scatter_job(links, source, mine, out, near, far, other):
    x, zl = links.x, links.zl

    def strip(p, h):
        return source.at[:, rows_at((p * 2 + h) * ROWS, ROWS)]

    local = strip
    if mine is not None:
        ahead, behind = lax.rem(x + 1, 4), lax.rem(x + 3, 4)
        places = [(behind, 0), (ahead, 1), (x, 0), (x, 1)]
        slots = [links.move(strip(*place), mine.at[i]) for i, place in enumerate(places)]

        def local(p, h):
            if p is x:
                return mine.at[2 + h]
            return mine.at[h]

    ring = ring_steps(links, strip, local, near, far, x, links.x_plus, links.x_minus)
    next(ring)
    yield
    if mine is not None:
        for i, slot in enumerate(slots):
            links.arrive(mine.at[i], slot)
    yield from ring
    yield from swap_steps(links, local, x, other, zl, links.z_shard)
    links.arrive(out, links.move(local(x, zl), out))


def token_gather_job(links, own, out, low_rows):
    mine = links.shard * ROWS
    nl, nh = low_rows, ROWS - low_rows
    z, xp, xm = links.z_shard, links.x_plus, links.x_minus

    def part(shard, first, count):
        return out.at[rows_at(shard * ROWS + first, count)]

    def forward(shard, first, count, device):
        return links.send(part(shard, first, count), part(shard, first, count), device)

    def near(step, flip):
        zl = 1 - links.zl if flip else links.zl
        return lax.rem(links.x + step, 4) * 2 + zl

    behind, ahead, across = near(3, False), near(1, False), near(2, False)
    behind_z, ahead_z, across_z, own_z = near(3, True), near(1, True), near(2, True), near(0, True)
    low, high = pl.ds(0, nl), pl.ds(nl, nh)
    z_low = links.send(own.at[low], part(links.shard, 0, nl), z)
    p_low = links.send(own.at[low], part(links.shard, 0, nl), xp)
    m_low = links.send(own.at[low], part(links.shard, 0, nl), xm)
    p_high = links.send(own.at[high], part(links.shard, nl, nh), xp)
    m_high = links.send(own.at[high], part(links.shard, nl, nh), xm)
    z_high = links.send(own.at[high], part(links.shard, nl, nh), z)
    kept = links.move(own, out.at[rows_at(mine, ROWS)])
    yield
    links.arrive(out.at[rows_at(mine, ROWS)], kept)
    links.arrive(part(own_z, 0, nl), z_low)
    p_z = forward(own_z, 0, nl, xp)
    m_z = forward(own_z, 0, nl, xm)
    links.arrive(part(behind, 0, nl), p_low)
    p_far0 = forward(behind, 0, nl // 2, xp)
    links.arrive(part(ahead, 0, nl), m_low)
    m_far0 = forward(ahead, nl // 2, nl // 2, xm)
    yield
    links.arrive(part(own_z, nl, nh), z_high)
    links.arrive(part(behind, nl, nh), p_high)
    z_behind = forward(behind, nl, nh, z)
    p_far1 = forward(behind, nl, nh // 2, xp)
    links.arrive(part(ahead, nl, nh), m_high)
    z_ahead = forward(ahead, nl, nh, z)
    m_far1 = forward(ahead, nl + nh // 2, nh // 2, xm)
    yield
    links.arrive(part(behind_z, 0, nl), p_z)
    p_far2 = forward(behind_z, 0, nl // 2, xp)
    links.arrive(part(ahead_z, 0, nl), m_z)
    m_far2 = forward(ahead_z, nl // 2, nl // 2, xm)
    links.arrive(part(across, nl, nh // 2), p_far1)
    z_far0 = forward(across, nl, nh // 2, z)
    links.arrive(part(across, nl + nh // 2, nh // 2), m_far1)
    z_far1 = forward(across, nl + nh // 2, nh // 2, z)
    links.arrive(part(behind_z, nl, nh), z_behind)
    links.arrive(part(ahead_z, nl, nh), z_ahead)
    yield
    links.arrive(part(across, 0, nl // 2), p_far0)
    links.arrive(part(across, nl // 2, nl // 2), m_far0)
    links.arrive(part(across_z, 0, nl // 2), p_far2)
    links.arrive(part(across_z, nl // 2, nl // 2), m_far2)
    links.arrive(part(across_z, nl, nh // 2), z_far0)
    links.arrive(part(across_z, nl + nh // 2, nh // 2), z_far1)


def weight_job(links, weight, out, spans):
    piece = rows_at((links.y * 2 + links.c) * 32, 32)
    arrivals = []
    for k in range(8):
        target = links.peer(k)
        for to, first, stride, width in spans:
            cols = pl.ds(pl.multiple_of(first + target * stride, 256), width)
            src, dst = weight.at[piece, cols], out.at[links.shard, piece, pl.ds(to, width)]
            slot = links.send(src, dst, (links.rep, target)) if k else links.move(src, dst)
            arrivals.append((slot, to, width))
    yield
    for slot, to, width in arrivals:
        links.arrive(out.at[0, piece, pl.ds(to, width)], slot)

    def strip(step, first, count):
        return out.at[:, rows_at((lax.rem(links.y + step, 4) * 2 + links.c) * 32 + first, count)]

    def forward(step, first, count, device):
        return links.send(strip(step, first, count), strip(step, first, count), device)

    plus = forward(0, 0, 32, links.y_plus)
    minus = forward(0, 0, 32, links.y_minus)
    given = [(forward(0, 0, 32, links.sibling), 32)]
    yield
    links.arrive(strip(3, 0, 32), plus)
    far0 = forward(3, 0, 16, links.y_plus)
    given.append((forward(3, 0, 32, links.sibling), 32))
    links.arrive(strip(1, 0, 32), minus)
    far1 = forward(1, 16, 16, links.y_minus)
    given.append((forward(1, 0, 32, links.sibling), 32))
    yield
    links.arrive(strip(2, 0, 16), far0)
    given.append((forward(2, 0, 16, links.sibling), 16))
    links.arrive(strip(2, 16, 16), far1)
    given.append((forward(2, 16, 16, links.sibling), 16))
    yield
    for slot, count in given:
        links.arrive(strip(0, 0, count), slot)


def exchange_columns(links, held, out, row, m, cols):
    waits = []
    for k in range(8):
        target = links.peer(k)
        for first, start, stride, width in cols:
            there = pl.ds(pl.multiple_of(start + links.shard * stride, 256), width)
            src = held.at[target, :, pl.ds(first, width)]
            dst = out.at[rows_at(row, m), there]
            slot = links.send(src, dst, (links.rep, target)) if k else links.move(src, dst)
            waits.append((slot, dst))
    return waits


def grad_job_z(links, grad, out, cols, m, got, near, far, other, ready=None):
    c, y, zh = links.c, links.y, links.zh
    count, _, width = grad.shape
    half, out_half = width // 2, out.shape[1] // 2

    def row(cc, yy, hh):
        return (cc * 8 + yy * 2 + hh) * m

    theirs = [lax.rem(y + step, 4) for step in (2, 1, 3, 0)]
    if ready is None:
        slots = [
            links.send(grad.at[:, rows_at(row(1 - c, p, 0), 2 * m)], got.at[:, rows_at(p * 2 * m, 2 * m)], links.sibling)
            for p in theirs
        ]
        yield
        for p, slot in zip(theirs, slots):
            links.arrive(got.at[:, rows_at(p * 2 * m, 2 * m)], slot)
    else:
        ready()
    add_into(grad.at[:, rows_at(c * 8 * m, 8 * m)], got)

    def held(p, h):
        return grad.at[:, rows_at(row(c, p, h), m)]

    slots = [links.send(held(p, 1 - zh), other.at[:, p], links.z_rep) for p in theirs]
    yield
    for p, slot in zip(theirs, slots):
        links.arrive(other.at[:, p], slot)
        add_into(held(p, zh), other.at[:, p])

    def side(p, h):
        return grad.at[:, rows_at(row(c, p, zh), m), pl.ds(h * half, half)]

    yield from ring_steps(links, side, side, near, far, y, links.y_plus, links.y_minus)

    def strip(yy, hh, n):
        return out.at[rows_at(row(c, yy, hh), n)]

    def forward(yy, hh, n, device):
        return links.send(strip(yy, hh, n), strip(yy, hh, n), device)

    def out_side(yy, h):
        return out.at[rows_at(row(c, yy, zh), m), pl.ds(h * out_half, out_half)]

    mine = strip(y, zh, m)
    if count == 1:
        links.arrive(mine, links.move(held(y, zh).at[0], mine))
    else:
        waits = exchange_columns(links, held(y, zh), out, row(c, y, zh), m, cols)
        yield
        for slot, dst in waits:
            links.arrive(dst, slot)
    e0 = forward(y, zh, m, links.y_plus)
    e1 = forward(y, zh, m, links.y_minus)
    za = forward(y, zh, m, links.z_rep)
    yield
    behind, ahead, across = lax.rem(y + 3, 4), lax.rem(y + 1, 4), lax.rem(y + 2, 4)
    links.arrive(strip(behind, zh, m), e0)
    f0 = links.send(out_side(behind, 0), out_side(behind, 0), links.y_plus)
    zb0 = forward(behind, zh, m, links.z_rep)
    links.arrive(strip(ahead, zh, m), e1)
    f1 = links.send(out_side(ahead, 1), out_side(ahead, 1), links.y_minus)
    zb1 = forward(ahead, zh, m, links.z_rep)
    yield
    links.arrive(out_side(across, 0), f0)
    links.arrive(out_side(across, 1), f1)
    zc = forward(across, zh, m, links.z_rep)
    links.arrive(strip(y, 1 - zh, m), za)
    given = [forward(y, 0, 2 * m, links.sibling)]
    yield
    links.arrive(strip(behind, 1 - zh, m), zb0)
    given.append(forward(behind, 0, 2 * m, links.sibling))
    links.arrive(strip(ahead, 1 - zh, m), zb1)
    given.append(forward(ahead, 0, 2 * m, links.sibling))
    yield
    links.arrive(strip(across, 1 - zh, m), zc)
    given.append(forward(across, 0, 2 * m, links.sibling))
    yield
    for slot in given:
        links.arrive(strip(y, 0, 2 * m), slot)


def grad_job(links, grad, out, cols, m, got, near, far, other, ready=None):
    c, y, zh = links.c, links.y, links.zh
    count = grad.shape[0]

    def row(cc, yy, hh):
        return (cc * 8 + yy * 2 + hh) * m

    theirs = [lax.rem(y + step, 4) for step in (2, 1, 3, 0)]
    if ready is None:
        slots = [
            links.send(grad.at[:, rows_at(row(1 - c, p, 0), 2 * m)], got.at[:, rows_at(p * 2 * m, 2 * m)], links.sibling)
            for p in theirs
        ]
        yield
        for p, slot in zip(theirs, slots):
            links.arrive(got.at[:, rows_at(p * 2 * m, 2 * m)], slot)
    else:
        ready()

    add_into(grad.at[:, rows_at(c * 8 * m, 8 * m)], got)
    def held(p, h):
        return grad.at[:, rows_at(row(c, p, h), m)]

    yield from ring_steps(links, held, held, near, far, y, links.y_plus, links.y_minus)
    yield from swap_steps(links, held, y, other, zh, links.z_rep)
    piece = held(y, zh)

    def strip(yy, hh, n):
        return out.at[rows_at(row(c, yy, hh), n)]

    def forward(yy, hh, n, device):
        return links.send(strip(yy, hh, n), strip(yy, hh, n), device)

    mine = strip(y, zh, m)
    if count == 1:
        links.arrive(mine, links.move(piece.at[0], mine))
    else:
        waits = exchange_columns(links, piece, out, row(c, y, zh), m, cols)
        yield
        for slot, dst in waits:
            links.arrive(dst, slot)
    a = forward(y, zh, m, links.z_rep)
    yield
    links.arrive(mine, a)
    e0 = forward(y, 0, 2 * m, links.y_plus)
    e1 = forward(y, 0, 2 * m, links.y_minus)
    given = [(forward(y, 0, 2 * m, links.sibling), 2 * m)]
    yield
    behind, ahead, across = lax.rem(y + 3, 4), lax.rem(y + 1, 4), lax.rem(y + 2, 4)
    links.arrive(strip(behind, 0, 2 * m), e0)
    f0 = forward(behind, 0, m, links.y_plus)
    given.append((forward(behind, 0, 2 * m, links.sibling), 2 * m))
    links.arrive(strip(ahead, 0, 2 * m), e1)
    f1 = forward(ahead, 1, m, links.y_minus)
    given.append((forward(ahead, 0, 2 * m, links.sibling), 2 * m))
    yield
    links.arrive(mine, f0)
    given.append((forward(across, 0, m, links.sibling), m))
    links.arrive(mine, f1)
    given.append((forward(across, 1, m, links.sibling), m))
    yield
    for slot, n in given:
        links.arrive(strip(y, 0, n), slot)


def vector_job(links, source, out, parts, acc, slots_y, other):
    a = links.move(source.at[links.shard], parts.at[links.shard])
    waits = [
        links.send(source.at[links.peer(k)], parts.at[links.shard], (links.rep, links.peer(k)))
        for k in range(1, 8)
    ]
    yield
    links.arrive(parts.at[0], a)
    for slot in waits:
        links.arrive(parts.at[0], slot)
    value = parts[0]
    for s in range(1, 8):
        value = value + parts[s]
    acc[0] = value
    a = links.send(acc.at[0], other.at[0], links.sibling)
    yield
    links.arrive(other.at[0], a)
    acc[1] = acc[0] + other[0]
    a = links.send(acc.at[1], other.at[1], links.z_rep)
    yield
    links.arrive(other.at[1], a)
    acc[2] = acc[1] + other[1]
    slots_y[links.y] = acc[2]
    there = slots_y.at[links.y]
    waits = [links.send(acc.at[2], there, d) for d in (links.y_plus, links.y_minus, links.y_far)]
    yield
    for slot in waits:
        links.arrive(there, slot)
    out[...] = (slots_y[0] + slots_y[1]) + (slots_y[2] + slots_y[3])


def step(*jobs):
    for job in jobs:
        next(job, None)


def run_jobs(*jobs):
    jobs = list(jobs)
    while jobs:
        jobs = [job for job in jobs if next(job, True) is None]


N_SEMS = 320
BACKWARD_ORDER = (
    "S0", "S1", "*lead", "out", "*sl1", "S0", "*sl2", "*ag", "S1", "*D", "D", "*E0", "E0", "D",
    "out", "S0", "*E1", "E1", "E0", "D", "S1", "*at1", "E1", "D", "S0", "*at2", "*key", "E1", "*A0",
    "A0", "E0", "*A1", "A1", "A0", "S1", "E1", "A1", "E0", "out", "D", "A0", "*A2", "A2", "S1",
    "A1", "*in1", "A2", "A0", "E0", "E1", "*in2", "in0", "S1", "*in3", "A2", "A1", "E0", "out", "D",
    "A0", "in0", "A2", "A1", "E1", "S0", "S1", "*in4", "in1", "A2", "E0", "S1", "*v", "vec", "A0",
    "D", "E1", "in0", "A1", "E0", "D", "E0", "S0", "D", "A0", "in1", "E1", "in0", "A1", "S0", "A2",
    "A0", "E0", "S0", "vec", "vec", "E0", "E1", "A2", "E1", "A1", "vec", "in1", "A0", "A0", "A2",
    "A1", "vec", "A1", "A2", "in1", "A2",
)
Z_FIRST = ("E0",)
FORWARD_ORDER = (
    "E", "V", "X", "A", "*t1", "*t2", "E", "V", "X", "X", "*n0", "E", "A", "E", "E", "X", "C",
    "*e0", "A", "*nm", "*nq", "X", "*em", "*eq", "*n2", "A", "C", "A", "*e2", "*p", "C", "*a0",
    "*a1", "*a2", "C", "*s3", "C", "*s2",
)


def follow(order, tasks, jobs):
    for name in order:
        if name[0] == "*":
            tasks[name[1:]]()
        else:
            next(jobs[name], None)
    run_jobs(*jobs.values())

ANY = pl.BlockSpec(memory_space=pl.ANY)
VMEM = pl.BlockSpec(memory_space=pltpu.VMEM)
SMEM = pl.BlockSpec(memory_space=pltpu.SMEM)


def sems(n):
    return [pltpu.SemaphoreType.DMA((n,)), pltpu.SemaphoreType.DMA((n,))]


def shape(*dims, kind=BF):
    return jax.ShapeDtypeStruct(dims, kind)


def small_job(links, small, out):
    slots = [links.send(small, out.at[links.shard], (links.rep, links.peer(k))) for k in range(1, 8)]
    slots.append(links.move(small, out.at[links.shard]))
    yield
    for slot in slots:
        links.arrive(out.at[0], slot)


def forward_kernel(
    tok, cot_own, we_own, wa_own, wd_in, ws_in, g_a, s_a, g_f, s_f, b_d, b_s, b_a, b_e, source, lengths,
    x_out, we_out, wa_out, cot_all, attend_out, feed_out, slope_out, q_out, k_out, v_out,
    prob_out, mixed_out, part_out, shrink_out, shrink_got, stats_keep, vec_keep, cosine_keep, sine_keep,
    send_sems, recv_sems, x, we3, wa3, wd, ws, attend_in, feed_in, act, slope, q, k, v, prob, mixed, part,
    cot, g_shrink, small, small_all, src, begin, total, stats_out, vec_out, cosine, sine,
):
    links = Links(send_sems, recv_sems)
    own = links.shard
    def pack():
        small[...] = jnp.zeros((16, 256), F32)
        row = 0
        for ref in (g_a, s_a, g_f, s_f, b_d, b_s, b_a, b_e):
            for first in range(0, ref.shape[0], 256):
                small[row : row + 1, :] = ref[pl.ds(first, 256)].astype(F32).reshape(1, 256)
                row += 1

    links.greet(
        [(links.rep, links.peer(p)) for p in range(1, 8)]
        + [links.sibling, links.y_plus, links.y_minus],
        pack,
    )
    expand = weight_job(links, we_own, we3, [(0, 0, FF_DEV, FF_DEV)])
    attend = weight_job(links, wa_own, wa3, [(p * HD, p * D, HD, HD) for p in range(3)])
    gather_x = token_gather_job(links, tok, x, 64)
    gather_cot = token_gather_job(links, cot_own, cot, 96)
    vectors = small_job(links, small, small_all)
    loads = []
    saves = []
    kept = {}

    def save(*pairs):
        for a, b in pairs:
            saves.append((links.move(a, b), b))

    def table_task(h):
        def run():
            if h == 0:
                loads.extend([links.move(wd_in, wd), links.move(ws_in, ws)])
                src[...] = jnp.broadcast_to(source[...].astype(F32), (128, GROUP)).T

            def tile(i, rows):
                here = src[rows, :]
                first = jnp.zeros_like(here)
                start = jnp.int32(0)
                for j in range(3):
                    start = start + lengths[0, j]
                    edge = start.astype(F32)
                    first = jnp.where(here >= edge, edge, first)
                begin[rows, :] = first
                lane = lax.broadcasted_iota(jnp.int32, here.shape, 1)
                pair = lax.rem(lane, ROT // 2).astype(F32)
                angle = (here - first) * jnp.exp(pair * (-2.0 * 9.210340371976184 / ROT))
                cosine[rows, :] = jnp.where(lane < ROT, jnp.cos(angle), 1.0)
                turned = jnp.sin(angle)
                sine[rows, :] = jnp.where(lane < ROT // 2, -turned, jnp.where(lane < ROT, turned, 0.0))

            span(2 * h, 2 * h + 2, 256, tile)
            if h == 1:
                save((cosine, cosine_keep), (sine, sine_keep))

        return run

    def pair_rows(hop, first, count):
        return rows_at(lax.rem(links.x + hop, 4) * 256 + first, count)

    def norm_task(hop):
        def run():
            if hop == 0:
                for s in range(8):
                    vec_out[:, s * 256 : (s + 1) * 256] = small_all[s, 0:8, :]
                pieces = []
                for p in range(3):
                    block = p * 8 + own
                    pieces.append(small_all[lax.div(block, 3), pl.ds(6 + lax.rem(block, 3), 1), :])
                kept["attend"] = jnp.concatenate(pieces, axis=1)
                kept["expand"] = jnp.concatenate([small_all[own, 9 + p : 10 + p, :] for p in range(4)], axis=1)

            def tile(i, carry):
                rows = pair_rows(hop, i * 128, 128)
                values = x[rows, :].astype(F32)
                mean = jnp.mean(values, axis=1, keepdims=True)
                center = values - mean
                inv = lax.rsqrt(jnp.mean(center * center, axis=1, keepdims=True) + EPSILON)
                normed = center * inv
                attend_in[rows, :] = (normed * vec_out[0:1, :] + vec_out[1:2, :]).astype(BF)
                feed_in[rows, :] = (normed * vec_out[2:3, :] + vec_out[3:4, :]).astype(BF)
                lane = lax.broadcasted_iota(jnp.int32, (128, 128), 1)
                stats_out[rows, :] = jnp.where(lane == 0, mean, inv)
                return carry

            lax.fori_loop(0, 2, tile, 0)
            if hop == 2:
                save((x, x_out), (attend_in, attend_out), (feed_in, feed_out), (stats_out, stats_keep), (vec_out, vec_keep))

        return run

    we, wa = we3.reshape(D, FF_DEV), wa3.reshape(D, 3 * HD)

    def expand_task(hop):
        def run():
            if hop == 0:
                save((we3, we_out))
            rows = pair_rows(hop, 0, 256)
            pre = dot(feed_in[rows, :], we[...], NN) + kept["expand"]
            below = 0.5 * (1.0 + lax.erf(pre * (0.5 ** 0.5)))
            act[rows, :] = (pre * below).astype(BF)
            density = jnp.exp(-0.5 * pre * pre) * 0.3989422804014327
            slope[rows, :] = (below + pre * density).astype(BF)
            if hop == 2:
                save((slope, slope_out))

        return run

    def shrink_task(hops):
        def run():
            pairs = [pair_rows(hop, 0, 256) for hop in hops]
            for rows in pairs:
                save((cot.at[rows], cot_all.at[rows]))

            def tile(i, here):
                for half in range(2):
                    cols = pl.ds(half * 1024, 1024)
                    value = dot(act[pairs[0], here], cot[pairs[0], cols], TN)
                    for rows in pairs[1:]:
                        value = value + dot(act[rows, here], cot[rows, cols], TN)
                    if len(pairs) > 1:
                        total[here, cols] = value
                    else:
                        g_shrink[0, here, cols] = (total[here, cols] + value).astype(BF)

            if len(pairs) > 1:
                tiles(FF_DEV, 256, tile)
                return
            for i in range(4):
                half = 1 - links.c if i < 2 else links.c
                here = pl.ds(pl.multiple_of(half * 512 + i % 2 * 256, 256), 256)
                tile(i, here)
                place = pl.ds(i % 2 * 256, 256)
                if i < 2:
                    slot = links.send(g_shrink.at[0, here], shrink_got.at[0, place], links.sibling)
                    saves.append((slot, shrink_got.at[0, place]))
                else:
                    save((g_shrink.at[0, here], shrink_out.at[0, place]))

        return run

    def project_task():
        save((wa3, wa_out))

        def tile(i, rows):
            triple = dot(attend_in[rows, :], wa[...], NN) + kept["attend"]
            cos, sin = cosine[rows, :], sine[rows, :]
            q[rows, :] = (turn(triple[:, :HD], cos, sin) * INV_ROOT).astype(BF)
            k[rows, :] = turn(triple[:, HD : 2 * HD], cos, sin).astype(BF)
            v[rows, :] = triple[:, 2 * HD :].astype(BF)

        tiles(GROUP, 256, tile)
        save((q, q_out), (k, k_out), (v, v_out))

    def attention_rows(rows):
        key_src = source[...].astype(F32)
        scores = dot(q[rows, :], k[...], NT)
        visible = (key_src >= begin[rows, 0:1]) & (key_src <= src[rows, 0:1])
        scores = jnp.where(visible, scores, NEG_FILL)
        weights = jnp.exp(scores - jnp.max(scores, axis=1, keepdims=True))
        return (weights * (1.0 / jnp.sum(weights, axis=1, keepdims=True))).astype(BF)

    def mix_rows(rows, weights):
        prob[rows, :] = weights
        mixed[rows, :] = dot(weights, v[...], NN).astype(BF)

    def out_rows(rows):
        total = dot(act[rows, :], ws[...], NN) + dot(mixed[rows, :], wd[...], NN)
        part[rows, :] = total.astype(BF)

    def attention_first():
        links.arrive(wd, loads[0])
        links.arrive(ws, loads[1])
        rows = pl.ds(0, 256)
        mix_rows(rows, attention_rows(rows))

    def attention_next():
        def tile(i, rows):
            weights = attention_rows(rows)
            out_rows(pl.ds(pl.multiple_of(i * 256 - 256, 256), 256))
            mix_rows(rows, weights)

        span(1, 4, 256, tile)
        save((prob, prob_out), (mixed, mixed_out))

    def out_last():
        out_rows(pl.ds(768, 256))
        save((part, part_out))

    tasks = {
        "t1": table_task(0), "t2": table_task(1), "p": project_task,
        "a0": attention_first, "a1": attention_next, "a2": out_last,
    }
    tasks["s3"] = shrink_task((0, 3, 1))
    tasks["s2"] = shrink_task((2,))
    for hop, name in ((0, "0"), (3, "m"), (1, "q"), (2, "2")):
        tasks["n" + name] = norm_task(hop)
        tasks["e" + name] = expand_task(hop)
    follow(FORWARD_ORDER, tasks, {"E": expand, "A": attend, "X": gather_x, "C": gather_cot, "V": vectors})
    for slot, ref in saves:
        links.arrive(ref, slot)
    links.close()


def forward(*args):
    big, wide, head = (GROUP, D), (GROUP, FF_DEV), (GROUP, HD)
    table = shape(GROUP, 128, kind=F32)
    return pl.pallas_call(
        forward_kernel,
        out_shape=(
            shape(*big), shape(8, 256, FF_DEV), shape(8, 256, 3 * HD), shape(*big),
            shape(*big), shape(*big), shape(*wide),
            shape(*head), shape(*head), shape(*head), shape(GROUP, GROUP), shape(*head), shape(*big),
            shape(1, 512, D), shape(1, 512, D), table, shape(8, D, kind=F32), table, table,
        ),
        in_specs=[ANY] * 6 + [VMEM] * 9 + [SMEM],
        out_specs=[ANY] * 19,
        scratch_shapes=sems(N_SEMS)
        + [
            pltpu.VMEM(dims, BF)
            for dims in (
                big, (8, 256, FF_DEV), (8, 256, 3 * HD), (HD, D), (FF_DEV, D), big, big, wide, wide,
                head, head, head, (GROUP, GROUP), head, big, big, (1, FF_DEV, D),
            )
        ]
        + [
            pltpu.VMEM((16, 256), F32),
            pltpu.VMEM((8, 16, 256), F32),
            pltpu.VMEM((GROUP, 128), F32),
            pltpu.VMEM((GROUP, 128), F32),
            pltpu.VMEM((FF_DEV, D), F32),
            pltpu.VMEM((GROUP, 128), F32),
            pltpu.VMEM((8, D), F32),
            pltpu.VMEM((GROUP, 128), F32),
            pltpu.VMEM((GROUP, 128), F32),
        ],
        compiler_params=pltpu.CompilerParams(
            collective_id=0, has_side_effects=True, vmem_limit_bytes=62 << 20
        ),
        name="forward",
    )(*args)


def backward_kernel(
    cot_in, shrink_in, shrink_got, slope_in, feed_in, attend_in, x_in, q_in, k_in, v_in, prob_in, mixed_in, part_in,
    we_in, wa_in, wd_in, ws_in, vec_in, stats_in, cosine_in, sine_in,
    o_shrink, o_expand0, o_expand1, o_attend, o_dense, r_out, r_in, o_vec,
    send_sems, recv_sems,
    rows_buf, we, norm_buf, act_buf, eg, wa, wd, q, k, v, prob, mixed, out_strips,
    g_shrink, g_expand, g_attend, g_dense, ag, tg, sums, vec_parts, vec, stats, cosine, sine, *scratch,
):
    links = Links(send_sems, recv_sems)
    take = iter(scratch)

    def grab(n):
        return [next(take) for _ in range(n)]

    def load(*pairs):
        return [(links.move(a, b), b) for a, b in pairs]

    def ready(loads):
        for slot, ref in loads:
            links.arrive(ref, slot)

    half = rows_at(links.c * 512, 512)
    shrink_scratch = [grab(4), grab(4)]
    loads = {}
    for h in range(2):
        cols = pl.ds(h * 1024, 1024)
        loads["S%d" % h] = load(
            (shrink_in.at[:, :, cols], g_shrink.at[:, half, cols]), (shrink_got.at[:, :, cols], shrink_scratch[h][0])
        )
    links.greet(
        [(links.rep, links.peer(p)) for p in range(1, 8)]
        + [links.sibling, links.z_rep, links.y_plus, links.y_minus, links.y_far]
    )
    cot = rows_buf.at[0]
    jobs = {}
    for h in range(2):
        cols = pl.ds(h * 1024, 1024)
        jobs["S%d" % h] = (grad_job, grad_job_z)["S%d" % h in Z_FIRST](
            links, g_shrink.at[:, :, cols], o_shrink.at[:, cols], None, 64, *shrink_scratch[h],
            lambda h=h: ready(loads["S%d" % h]),
        )
    for h, out in ((0, o_expand0), (1, o_expand1)):
        jobs["E%d" % h] = (grad_job, grad_job_z)["E%d" % h in Z_FIRST](
            links, g_expand.at[:, :, pl.ds(h * 512, 512)], out, [(0, 0, 512, 512)], 16, *grab(4)
        )
    for p in range(3):
        jobs["A%d" % p] = grad_job(
            links, g_attend.at[:, :, pl.ds(p * HD, HD)], o_attend.at[:, pl.ds(p * D, D)],
            [(0, 0, HD, HD)], 16, *grab(4)
        )
    jobs["D"] = grad_job(links, g_dense, o_dense, None, 16, *grab(4))
    jobs["out"] = token_scatter_job(links, part_in, out_strips, r_out, *grab(3))
    for h in range(2):
        cols = pl.ds(h * 1024, 1024)
        jobs["in%d" % h] = token_scatter_job(
            links, rows_buf.at[:, :, cols], None, r_in.at[:, :, cols], *grab(3)
        )
    ones = jnp.ones((8, GROUP), BF)

    kept = {}

    def lead_task():
        loads["second"] = load((cot_in, rows_buf.at[0]), (slope_in, eg), (ws_in, norm_buf))
        loads["tables"] = load((vec_in, vec), (stats_in, stats), (cosine_in, cosine), (sine_in, sine))

    def slope_task(h):
        def run():
            if h == 0:
                ready(loads["second"])
                loads["third"] = load((wd_in, wd), (mixed_in, mixed))
                loads["fourth"] = load((q_in, q), (k_in, k), (v_in, v), (prob_in, prob))

            def tile(i, rows):
                grad = dot(cot[rows, :], norm_buf[...], NT)
                eg[rows, :] = (grad * eg[rows, :].astype(F32)).astype(BF)

            span(2 * h, 2 * h + 2, 256, tile)
            if h == 1:
                loads["feed"] = load((feed_in, norm_buf))

        return run

    def attended_task():
        ready(loads["third"])

        def tile(i, rows):
            ag[rows, :] = dot(cot[rows, :], wd[...], NT).astype(BF)

        tiles(GROUP, 256, tile)

    def dense_task():
        for half in range(2):
            cols = pl.ds(half * 1024, 1024)
            g_dense[0, :, cols] = dot(mixed[...], cot[:, cols], TN).astype(BF)
        sums[4:5, :] = dot(ones, cot[...], NN)[0:1]
        loads["x"] = load((x_in, cot), (we_in, we), (wa_in, wa))

    def expand_task(h):
        def run():
            if h == 0:
                ready(loads["feed"])
            cols = pl.ds(h * 512, 512)

            def tile(i, rows):
                s = i * 2
                both = dot(norm_buf[:, rows], eg[:, cols], TN).astype(BF)
                g_expand[s, :, cols] = both[:256]
                g_expand[s + 1, :, cols] = both[256:]

            tiles(D, 512, tile)
            if h == 1:
                loads["attend"] = load((attend_in, norm_buf))
                kept["expand"] = dot(ones, eg[...], NN)[0:1]

        return run

    def attention_task(h):
        def run():
            if h == 0:
                ready(loads["fourth"] + loads["tables"])

            def tile(i, rows):
                grad = dot(ag[rows, :], v[...], NT)
                weights = prob[rows, :].astype(F32)
                inner = jnp.sum(weights * grad, axis=1, keepdims=True)
                score_grad = (weights * (grad - inner)).astype(BF)
                act_buf[rows, :] = score_grad
                query_grad = dot(score_grad, k[...], NN) * INV_ROOT
                tg[rows, 0:HD] = turn(query_grad, cosine[rows, :], -sine[rows, :]).astype(BF)

            span(4 * h, 4 * h + 4, 128, tile)

        return run

    def key_task():
        def tile(i, rows):
            key_grad = dot(act_buf[:, rows], q[...], TN)
            tg[rows, HD : 2 * HD] = turn(key_grad, cosine[rows, :], -sine[rows, :]).astype(BF)
            tg[rows, 2 * HD :] = dot(prob[:, rows], ag[...], TN).astype(BF)

        tiles(GROUP, 256, tile)

    def attend_task(p):
        def run():
            if p == 0:
                ready(loads["attend"])
            cols = pl.ds(p * HD, HD)

            def tile(i, rows):
                s = i * 2
                both = dot(norm_buf[:, rows], tg[:, cols], TN).astype(BF)
                g_attend[s, :, cols] = both[:256]
                g_attend[s + 1, :, cols] = both[256:]

            tiles(D, 512, tile)
            if p == 2:
                kept["attend"] = dot(ones, tg[...], NN)[0:1]

        return run

    def input_task(h):
        def run():
            if h == 0:
                ready(loads["x"])
                sums[0:4, :] = jnp.zeros((4, D), F32)

            def tile(i, carry):
                rows = pl.ds(pl.multiple_of((h % 2 * 2 + i // 2) * 256, 256), 256)
                cols = pl.ds(pl.multiple_of((h // 2 * 2 + lax.rem(i, 2)) * 512, 512), 512)
                normed = (cot[rows, cols].astype(F32) - stats[rows, 0:1]) * stats[rows, 1:2]
                grad = dot(tg[rows, :], wa[cols, :], NT)
                sums[0:1, cols] += jnp.sum(grad * normed, axis=0, keepdims=True)
                sums[1:2, cols] += jnp.sum(grad, axis=0, keepdims=True)
                combined = grad * vec[0:1, cols]
                grad = dot(eg[rows, :], we[cols, :], NT)
                sums[2:3, cols] += jnp.sum(grad * normed, axis=0, keepdims=True)
                sums[3:4, cols] += jnp.sum(grad, axis=0, keepdims=True)
                cot[rows, cols] = (combined + grad * vec[2:3, cols]).astype(BF)
                return carry

            lax.fori_loop(0, 4, tile, 0)

        return run

    def vector_task():
        own = links.shard
        for s in range(8):
            vec_parts[s] = jnp.zeros((16, 256), F32)
        for p in range(3):
            block = p * 8 + own
            vec_parts[lax.div(block, 3), pl.ds(lax.rem(block, 3), 1), :] = kept["attend"][:, p * HD : (p + 1) * HD]
        for p in range(4):
            vec_parts[own, 3 + p : 4 + p, :] = kept["expand"][:, p * 256 : (p + 1) * 256]
        for s in range(8):
            vec_parts[s, 7:11, :] = sums[0:4, s * 256 : (s + 1) * 256]
        vec_parts[own, 11:12, :] = sums[4:5, pl.ds(pl.multiple_of(own * 256, 256), 256)]

    jobs["vec"] = vector_job(links, vec_parts, o_vec, *grab(4))
    tasks = {
        "lead": lead_task, "sl1": slope_task(0), "sl2": slope_task(1),
        "ag": attended_task, "D": dense_task, "E0": expand_task(0), "E1": expand_task(1),
        "at1": attention_task(0), "at2": attention_task(1), "key": key_task,
        "A0": attend_task(0), "A1": attend_task(1), "A2": attend_task(2),
        "in1": input_task(0), "in2": input_task(1), "in3": input_task(2), "in4": input_task(3),
        "v": vector_task,
    }
    follow(BACKWARD_ORDER, tasks, jobs)
    links.close()


def grad_scratch(s, m, n, name=""):
    dims = ((2, s, 2, m, n), (2, s, m, n), (s, m, n))
    if name in Z_FIRST:
        dims = ((2, s, 2, m, n // 2), (2, s, m, n // 2), (s, 4, m, n))
    return [pltpu.VMEM((s, 8 * m, n), BF)] + [pltpu.VMEM(d, BF) for d in dims]


def token_scratch(width):
    return [
        pltpu.VMEM((2, 1, 2, ROWS, width), BF),
        pltpu.VMEM((2, 1, ROWS, width), BF),
        pltpu.VMEM((1, ROWS, width), BF),
    ]


def backward(*args):
    big, wide, head = (GROUP, D), (GROUP, FF_DEV), (GROUP, HD)
    return pl.pallas_call(
        backward_kernel,
        out_shape=(
            shape(FF_DEV, D), shape(256, 8 * 512), shape(256, 8 * 512), shape(256, 3 * D), shape(256, D),
            shape(1, ROWS, D), shape(1, ROWS, D), shape(16, 256, kind=F32),
        ),
        in_specs=[ANY] * 21,
        out_specs=[ANY] * 7 + [VMEM],
        scratch_shapes=sems(N_SEMS)
        + [
            pltpu.VMEM(dims, BF)
            for dims in (
                (1, *big), (D, FF_DEV), big, wide, wide, (D, 3 * HD), (HD, D),
                head, head, head, (GROUP, GROUP), head, (4, 1, ROWS, D),
                (1, FF_DEV, D), (8, 256, FF_DEV), (8, 256, 3 * HD), (1, 256, D), head, (GROUP, 3 * HD),
            )
        ]
        + [pltpu.VMEM((8, D), F32), pltpu.VMEM((8, 16, 256), F32), pltpu.VMEM((8, D), F32)]
        + [pltpu.VMEM((GROUP, 128), F32)] * 3
        + grad_scratch(1, 64, 1024, "S0")
        + grad_scratch(1, 64, 1024, "S1")
        + grad_scratch(8, 16, 512, "E0")
        + grad_scratch(8, 16, 512, "E1")
        + grad_scratch(8, 16, HD) * 3
        + grad_scratch(1, 16, D)
        + token_scratch(D)
        + token_scratch(1024) * 2
        + [
            pltpu.VMEM((8, 16, 256), F32),
            pltpu.VMEM((3, 16, 256), F32),
            pltpu.VMEM((4, 16, 256), F32),
            pltpu.VMEM((2, 16, 256), F32),
        ],
        compiler_params=pltpu.CompilerParams(
            collective_id=1, has_side_effects=True, vmem_limit_bytes=64 << 20
        ),
        name="backward",
    )(*args)


def finish_kernel(
    shrink, expand0, expand1, attend, dense, branch, combined, tok, cot, vec, sums,
    layer_out, tokens_grad, g_attend, b_attend, g_dense, b_dense, g_expand, b_expand, g_shrink, b_shrink,
    gain_a, shift_a, gain_f, shift_f,
):
    g_shrink[...] = shrink[...].astype(F32)
    for s in range(8):
        for h, half in enumerate((expand0, expand1)):
            g_expand[:, (2 * s + h) * 512 : (2 * s + h + 1) * 512] = half[:, s * 512 : (s + 1) * 512].astype(F32)
    g_attend[...] = attend[...].astype(F32)
    g_dense[...] = dense[...].astype(F32)
    values = tok[...].astype(F32)
    layer_out[...] = (values + branch[0].astype(F32) + vec[4:5, :] + vec[5:6, :]).astype(BF)
    center = values - jnp.mean(values, axis=1, keepdims=True)
    inv = lax.rsqrt(jnp.mean(center * center, axis=1, keepdims=True) + EPSILON)
    normed = center * inv
    grad = combined[0].astype(F32)
    mean = jnp.mean(grad, axis=1, keepdims=True)
    slant = jnp.mean(grad * normed, axis=1, keepdims=True)
    tokens_grad[...] = cot[...].astype(F32) + (grad - mean - normed * slant) * inv

    @pl.when(pl.program_id(0) == 0)
    def _():
        for ref, first in ((b_attend, 0), (b_expand, 3), (gain_a, 7), (shift_a, 8), (gain_f, 9), (shift_f, 10),
                           (b_dense, 11), (b_shrink, 11)):
            for i in range(ref.shape[0] // 256):
                ref[pl.ds(i * 256, 256)] = sums[first + i : first + i + 1, :].reshape(256)


def finish(*args):
    steps = 2

    def rows(n, width):
        return pl.BlockSpec((n // steps, width), lambda i: (i, 0))

    def part(n, width):
        return pl.BlockSpec((1, n // steps, width), lambda i: (0, i, 0))

    def whole(*dims):
        return pl.BlockSpec(dims, lambda i: (0,) * len(dims))

    weights = [rows(256, 3 * D), rows(256, D), rows(256, 8 * FF_DEV), rows(FF_DEV, D)]
    return pl.pallas_call(
        finish_kernel,
        grid=(steps,),
        out_shape=(
            shape(ROWS, D), shape(ROWS, D, kind=F32),
            shape(256, 3 * D, kind=F32), shape(768, kind=F32), shape(256, D, kind=F32), shape(256, kind=F32),
            shape(256, 8 * FF_DEV, kind=F32), shape(1024, kind=F32), shape(FF_DEV, D, kind=F32),
            *[shape(256, kind=F32)] * 5,
        ),
        in_specs=[weights[3], rows(256, 4096), rows(256, 4096), weights[0], weights[1], part(ROWS, D), part(ROWS, D)]
        + [rows(ROWS, D)] * 2
        + [whole(8, D), whole(16, 256)],
        out_specs=[
            rows(ROWS, D), rows(ROWS, D), weights[0], whole(768), weights[1], whole(256), weights[2],
            whole(1024), weights[3], *[whole(256)] * 5,
        ],
        compiler_params=pltpu.CompilerParams(vmem_limit_bytes=60 << 20),
        name="finish",
    )(*args)


def per_device(
    tokens,
    out_cotangent,
    attend_weight,
    attend_bias,
    dense_weight,
    dense_bias,
    expand_weight,
    expand_bias,
    shrink_weight,
    shrink_bias,
    attend_gain,
    attend_shift,
    feed_gain,
    feed_shift,
    lengths,
    slot_source,
):
    (
        x, we, wa, cot, attend_in, feed_in, slope, q, k, v, prob, mixed, part, shrink, shrink_got,
        stats, vec, cosine, sine,
    ) = forward(
        tokens, out_cotangent, expand_weight, attend_weight, dense_weight, shrink_weight,
        attend_gain, attend_shift, feed_gain, feed_shift, dense_bias, shrink_bias, attend_bias, expand_bias,
        slot_source, lengths,
    )
    we, wa = we.reshape(D, FF_DEV), wa.reshape(D, 3 * HD)
    (shrink_sum, expand0, expand1, attend_sum, dense_sum, branch_sum, own_combined, sums) = backward(
        cot, shrink, shrink_got, slope, feed_in, attend_in, x, q, k, v, prob, mixed, part.reshape(1, GROUP, D),
        we, wa, dense_weight, shrink_weight, vec, stats, cosine, sine,
    )
    return tuple(
        finish(
            shrink_sum, expand0, expand1, attend_sum, dense_sum, branch_sum, own_combined,
            tokens, out_cotangent, vec, sums,
        )
    )


def solution(mesh):
    rows, split, whole = P(("rep", "shard"), None), P("shard"), P("shard", None)
    return jax.shard_map(
        per_device,
        mesh=mesh,
        in_specs=(rows, rows)
        + (whole, split) * 4
        + (split,) * 4
        + (P("rep", None), P("rep", None)),
        out_specs=(rows, rows) + (whole, split) * 4 + (split,) * 4,
        check_vma=False,
    )
```

profile of v0, /device:TPU:1, one launch (start us, length us, event | category | flops | bytes accessed | tf_op | source)
XLA Modules:
  0.0 223.4 jit_solution(11499552966547841651)
XLA Ops:
  0.6 89.5 %forward.1 = (bf16[1024,2048]{1,0:T(8,128)(2,1)}, bf16[8,256,1024]{2,1,0:T(8,128)(2,1)}, bf16[8,256,768]{2,1,0:T(8,128)(2,1)}, bf16[1024,2048]{1,0:T(8,128)(2,1)...) custom-call(bf16[128,2048]{1,0:T(8,128)(2,1)} %tok.3, ...), custom_call_target="tpu_custom_call" | custom-call | tf_op jit(solution)/shard_map/forward/pallas_call | solution.py:749
  90.2 118.7 %backward.1 = (bf16[1024,2048]{1,0:T(8,128)(2,1)}, bf16[256,4096]{1,0:T(8,128)(2,1)}, bf16[256,4096]{1,0:T(8,128)(2,1)}, bf16[256,6144]{1,0:T(8,128)(2,1)}, bf16...) custom-call(bf16[1024,2048]{1,0:T(8,128)(2,1)} %get-tuple-element.41.c, ...), custom_call_target="tpu_custom_call" | custom-call | tf_op jit(solution)/shard_map/backward/pallas_call | solution.py:1012
  208.8 14.4 %finish.1 = (bf16[128,2048]{1,0:T(8,128)(2,1)}, f32[128,2048]{1,0:T(8,128)}, f32[256,6144]{1,0:T(8,128)}, f32[768]{0:T(1024)}, f32[256,2048]{1,0:T(8,128)}, /*in...) custom-call(bf16[1024,2048]{1,0:T(8,128)(2,1)} %get-tuple-element.60, ...), custom_call_target="tpu_custom_call" | custom-call | tf_op jit(solution)/shard_map/finish/pallas_call | solution.py:1094
where the time goes:
time: 224 us; the launch traced here: 223 us
  Pallas kernels  223 us (100%)
    pallas_call x1, Pallas kernels, backward(): pl.pallas_call(backward_kernel, out_shape=(shape(FF_DEV, D), shape(256, 8...  119 us
    pallas_call x1, Pallas kernels, forward(): pl.pallas_call(forward_kernel, out_shape=(shape(*big), shape(8, 256, FF_D...  89.5 us
    pallas_call x1, Pallas kernels, finish(): pl.pallas_call(finish_kernel, grid=(steps,), out_shape=(shape(ROWS, D), s...  14.4 us

commit v1 on v0

--- a/solution.py
+++ b/solution.py
@@ -471,7 +471,8 @@
     yield
     for slot in waits:
         links.arrive(there, slot)
-    out[...] = (slots_y[0] + slots_y[1]) + (slots_y[2] + slots_y[3])
+    parts[0] = (slots_y[0] + slots_y[1]) + (slots_y[2] + slots_y[3])
+    links.arrive(out, links.move(parts.at[0], out))
 
 
 def step(*jobs):
@@ -500,7 +501,7 @@
 FORWARD_ORDER = (
     "E", "V", "X", "A", "*t1", "*t2", "E", "V", "X", "X", "*n0", "E", "A", "E", "E", "X", "C",
     "*e0", "A", "*nm", "*nq", "X", "*em", "*eq", "*n2", "A", "C", "A", "*e2", "*p", "C", "*a0",
-    "*a1", "*a2", "C", "*s3", "C", "*s2",
+    "*a1", "C", "*a2", "*s3", "C", "*s2",
 )
 
 
@@ -1016,7 +1017,7 @@
             shape(1, ROWS, D), shape(1, ROWS, D), shape(16, 256, kind=F32),
         ),
         in_specs=[ANY] * 21,
-        out_specs=[ANY] * 7 + [VMEM],
+        out_specs=[ANY] * 8,
         scratch_shapes=sems(N_SEMS)
         + [
             pltpu.VMEM(dims, BF)

time: 224 us -> 223 us (level)
  no operation moved by 1% of the time
where the time goes in v1:
time: 223 us
  Pallas kernels  222 us (100%)
    pallas_call x1, Pallas kernels, backward(): pl.pallas_call(backward_kernel, out_shape=(shape(FF_DEV, D), shape(256, 8...  119 us
    pallas_call x1, Pallas kernels, forward(): pl.pallas_call(forward_kernel, out_shape=(shape(*big), shape(8, 256, FF_D...  88.8 us
    pallas_call x1, Pallas kernels, finish(): pl.pallas_call(finish_kernel, grid=(steps,), out_shape=(shape(ROWS, D), s...  14.4 us

profile of v1, /device:TPU:1, one launch (start us, length us, event | category | flops | bytes accessed | tf_op | source)
XLA Modules:
  0.0 222.7 jit_solution(1453546186737862665)
XLA Ops:
  0.6 88.8 %forward.1 = (bf16[1024,2048]{1,0:T(8,128)(2,1)}, bf16[8,256,1024]{2,1,0:T(8,128)(2,1)}, bf16[8,256,768]{2,1,0:T(8,128)(2,1)}, bf16[1024,2048]{1,0:T(8,128)(2,1)...) custom-call(bf16[128,2048]{1,0:T(8,128)(2,1)} %tok.3, ...), custom_call_target="tpu_custom_call" | custom-call | tf_op jit(solution)/shard_map/forward/pallas_call | solution.py:750
  89.5 118.6 %backward.1 = (bf16[1024,2048]{1,0:T(8,128)(2,1)}, bf16[256,4096]{1,0:T(8,128)(2,1)}, bf16[256,4096]{1,0:T(8,128)(2,1)}, bf16[256,6144]{1,0:T(8,128)(2,1)}, bf16...) custom-call(bf16[1024,2048]{1,0:T(8,128)(2,1)} %get-tuple-element.41.c, ...), custom_call_target="tpu_custom_call" | custom-call | tf_op jit(solution)/shard_map/backward/pallas_call | solution.py:1013
  208.1 14.4 %finish.1 = (bf16[128,2048]{1,0:T(8,128)(2,1)}, f32[128,2048]{1,0:T(8,128)}, f32[256,6144]{1,0:T(8,128)}, f32[768]{0:T(1024)}, f32[256,2048]{1,0:T(8,128)}, /*in...) custom-call(bf16[1024,2048]{1,0:T(8,128)(2,1)} %get-tuple-element.60, ...), custom_call_target="tpu_custom_call" | custom-call | tf_op jit(solution)/shard_map/finish/pallas_call | solution.py:1095
